TPU v7x, 32 devices: a whole 2x2x4 slice. The times are simulated.
32 devices in a mesh: groups: 2 (over x), seq: 8 (over z, y), heads: 2 (over core).
Axes of the slice: x: 2, y: 2, z: 4, core: 2. Of those that a mesh axis runs over, the one named last changes fastest.
Arguments:
- x_in: bfloat16 [2048, 8192], P(('groups', 'seq'), 'heads'), parts along dimension 0, may hold values from -6 to 6
- z_in: bfloat16 [2048, 8192], P(('groups', 'seq'), 'heads'), parts along dimension 0, may hold values from -6 to 6
- bc_in: bfloat16 [2048, 2, 512], P(('groups', 'seq'), None, 'heads'), parts along dimension 0, may hold values from -1.25 to 1.25
- conv_x_weight: bfloat16 [4, 8192], P(None, 'heads'), may hold values from -3 to 3
- conv_x_bias: float32 [8192], P('heads'), may hold values from -3 to 3
- conv_bc_weight: bfloat16 [4, 2, 512], P(None, None, 'heads'), may hold values from -3 to 3
- conv_bc_bias: float32 [2, 512], P(None, 'heads'), may hold values from -0.625 to 0.625
- dt_raw: bfloat16 [2048, 128], P(('groups', 'seq'), 'heads'), parts along dimension 0, may hold values from -3 to 3
- dt_bias: float32 [128], P('heads'), may hold values from -1 to 0.5
- decay: float32 [128], P('heads'), may hold values from 1.953125e-05 to 0.05
- skip_d: float32 [128], P('heads'), may hold values from 0.5 to 1.5
- norm_gain: float32 [8192], P('heads'), may hold values from 0.1 to 1.9
- lengths: int32 [16], P('groups'), parts along dimension 0, may hold values from 1 to 512, 1024 in all
Outputs:
- mixed: bfloat16 [2048, 8192], P(('groups', 'seq'), 'heads'), parts along dimension 0
There are 2 independent parts, one for each index of `groups`. A program takes and returns all parts, laid end to end along the dimension named above; an argument that names none is the same for every part. Nothing has to cross between parts.
Inputs may be any that keep to these rules, and one draw needn't show every extreme that they name: `lengths`: 8 token counts that sum to 1024; the longest rollout has exactly 512 tokens.
All inputs are finite; a program needn't handle non-finite values.
Results may differ from a plain program's by a relative error of at most 0.0098.
Values may be sent and summed in bfloat16 or wider, within the bound.
A program may use at most 192 MiB of HBM per device.

v0:
```python
import jax
import jax.numpy as jnp
from jax import lax
from jax.sharding import PartitionSpec as P

HEAD_DIM = 64
STATE = 128
BLOCK = 128


def shifted(block, axis, distance):
    devices = range(lax.axis_size(axis))
    route = [(i - distance, i) for i in devices if i - distance in devices]
    return lax.ppermute(block, axis, route)


def prefix_2(x, axis, combine, identity):
    peers, position = (lax.axis_size(axis), lax.axis_index(axis))
    everything = jax.tree.map(lambda part: lax.all_gather(part, axis), x)
    start = jax.tree.map(
        lambda part, zero: jnp.broadcast_to(jnp.asarray(zero, part.dtype), part.shape), x, identity
    )

    def step(k, before):
        reached = k < position
        new = combine(before, jax.tree.map(lambda part: part[k], everything))
        return jax.tree.map(lambda a, b: jnp.where(reached, a, b), new, before)

    return lax.fori_loop(0, peers, step, start)


def seg_ids(ends, pos):
    count = jnp.sum((ends[None, :] <= pos[:, None]).astype(jnp.int32), axis=1)
    return jnp.where(pos >= 0, count, -1)


def conv_act(extended, weight, bias, keep):
    rows = keep.shape[1]
    total = bias
    for k in range(weight.shape[0]):
        piece = extended[k : k + rows].astype(jnp.float32) * weight[k].astype(jnp.float32)
        flag = keep[k].reshape((rows,) + (1,) * (extended.ndim - 1))
        total = total + jnp.where(flag, piece, 0.0)
    return jax.nn.silu(total).astype(jnp.bfloat16)


def contract(form, left, right):
    return jnp.einsum(form, left, right, preferred_element_type=jnp.float32)


def block_terms(xs, rates, decay, bmat, cmat, seg, prev_seg, block):
    count, heads, hdim = xs.shape
    groups, state = (bmat.shape[1], bmat.shape[2])
    per = heads // groups
    blocks = count // block
    xb = xs.reshape(blocks, block, groups, per, hdim)
    rate_b = rates.reshape(blocks, block, groups, per)
    cum = jnp.cumsum(-rate_b * decay.reshape(groups, per), axis=1)
    segb = seg.reshape(blocks, block)
    bb = bmat.reshape(blocks, block, groups, state)
    cb = cmat.reshape(blocks, block, groups, state)
    scores = contract("btgn,bsgn->bgts", cb, bb)
    order = jnp.arange(block)
    mask = (segb[:, :, None] == segb[:, None, :]) & (order[:, None] >= order[None, :])
    cum_t = jnp.transpose(cum, (0, 2, 3, 1))
    diff = cum_t[..., :, None] - cum_t[..., None, :]
    mask5 = mask[:, None, None]
    decays = jnp.where(mask5, jnp.exp(jnp.where(mask5, diff, 0.0)), 0.0)
    rate_t = jnp.transpose(rate_b, (0, 2, 3, 1))
    weights = (decays * scores[:, :, None] * rate_t[..., None, :]).astype(jnp.bfloat16)
    inner = contract("bgkts,bsgkp->btgkp", weights, xb)
    last = cum[:, -1]
    same_end = segb == segb[:, -1:]
    to_end = jnp.where(same_end[:, :, None, None], jnp.exp(last[:, None] - cum), 0.0) * rate_b
    scaled = (to_end[..., None] * xb.astype(jnp.float32)).astype(jnp.bfloat16)
    states = contract("bsgn,bsgkp->bgknp", bb, scaled)
    live = segb == prev_seg[:, None]
    carry = jnp.where(live[:, -1][:, None, None], jnp.exp(last), 0.0)
    entry = jnp.where(live[:, :, None, None], jnp.exp(cum), 0.0)
    return (inner, states, carry, entry, cb, xb)


def combine(earlier, later):
    return (earlier[0] * later[0], later[0][..., None, None] * earlier[1] + later[1])


def prefix_blocks(carry, states):
    return lax.associative_scan(combine, (carry, states), axis=0)


def finish(pieces, prefix, skip, start):
    inner, states, carry, entry, cb, xb = pieces
    blocks, block, groups, per, hdim = xb.shape
    lead_g = jnp.concatenate([jnp.ones_like(prefix[0]), prefix[0][:-1]], axis=0)
    lead_s = jnp.concatenate([jnp.zeros_like(prefix[1]), prefix[1][:-1]], axis=0)
    entering = (lead_s + lead_g[..., None, None] * start[None]).astype(jnp.bfloat16)
    outer = contract("btgn,bgknp->btgkp", cb, entering) * entry[..., None]
    total = inner + outer + skip.reshape(groups, per)[:, :, None] * xb.astype(jnp.float32)
    return total.reshape(blocks * block, groups * per, hdim).astype(jnp.bfloat16)


def gated_norm(y, gate, gain, gsize):
    rows, width = y.shape
    mixed = y.astype(jnp.float32) * jax.nn.silu(gate.astype(jnp.float32))
    grouped = mixed.reshape(rows, width // gsize, gsize)
    meansq = jnp.mean(grouped * grouped, axis=-1, keepdims=True)
    normed = (grouped * lax.rsqrt(meansq + 1e-05)).reshape(rows, width)
    return (normed * gain).astype(jnp.bfloat16)


def shards(
    x_in,
    z_in,
    bc_in,
    conv_x_weight,
    conv_x_bias,
    conv_bc_weight,
    conv_bc_bias,
    dt_raw,
    dt_bias,
    decay,
    skip_d,
    norm_gain,
    lengths,
):
    rows = x_in.shape[0]
    shard = lax.axis_index("seq")
    heads_local = dt_raw.shape[1]
    groups_local = bc_in.shape[2] // STATE
    ends = jnp.cumsum(lengths)
    width = conv_x_weight.shape[0]
    edge_x, edge_bc = shifted((x_in[rows - width + 1 :], bc_in[rows - width + 1 :]), "seq", 1)
    position = shard * rows + jnp.arange(rows, dtype=jnp.int32)
    own = seg_ids(ends, position)
    keep = jnp.stack([seg_ids(ends, position - (width - 1) + k) == own for k in range(width)])
    xc = conv_act(jnp.concatenate([edge_x, x_in], axis=0), conv_x_weight, conv_x_bias, keep)
    bcc = conv_act(jnp.concatenate([edge_bc, bc_in], axis=0), conv_bc_weight, conv_bc_bias, keep)
    xh = xc.reshape(rows, heads_local, HEAD_DIM)
    rates = jax.nn.softplus(dt_raw.astype(jnp.float32) + dt_bias)
    bmat = bcc[:, 0].reshape(rows, groups_local, STATE)
    cmat = bcc[:, 1].reshape(rows, groups_local, STATE)
    prev_seg = seg_ids(ends, shard * rows + jnp.arange(rows // BLOCK, dtype=jnp.int32) * BLOCK - 1)
    pieces = block_terms(xh, rates, decay, bmat, cmat, own, prev_seg, BLOCK)
    prefix = prefix_blocks(pieces[2], pieces[1])
    identity = (jnp.ones_like(prefix[0][0]), jnp.zeros_like(prefix[1][0]))
    before = prefix_2((prefix[0][-1], prefix[1][-1]), "seq", combine, identity)
    y = finish(pieces, prefix, skip_d, before[1])
    gsize = heads_local * HEAD_DIM // groups_local
    return gated_norm(y.reshape(rows, heads_local * HEAD_DIM), z_in, norm_gain, gsize)


def solution(mesh):
    return jax.shard_map(
        shards,
        mesh=mesh,
        in_specs=(
            P(("groups", "seq"), "heads"),
            P(("groups", "seq"), "heads"),
            P(("groups", "seq"), None, "heads"),
            P(None, "heads"),
            P("heads"),
            P(None, None, "heads"),
            P(None, "heads"),
            P(("groups", "seq"), "heads"),
            P("heads"),
            P("heads"),
            P("heads"),
            P("heads"),
            P("groups"),
        ),
        out_specs=P(("groups", "seq"), "heads"),
        check_vma=False,
    )
```

profile of v0, /device:TPU:30, one launch (start us, length us, event | category | flops | bytes accessed | tf_op | source)
XLA Modules:
  0.0 357.2 jit_solution(2412453798349976921)
XLA Ops:
  6.5 0.9 slice.63
  7.4 1.3 collective-permute-start
  8.7 0.7 slice.71
  9.6 1.3 collective-permute-start.1
  10.9 0.8 reduce-window.4
  11.8 0.6 fusion.37
  13.7 1.6 slice_convert_fusion.3
  15.9 0.8 compare_select_fusion
  16.9 0.7 mul.277
  17.8 1.2 slice_bitcast_fusion
  19.7 0.7 bitcast_convert_fusion.3
  20.5 1.6 copy.85
  23.4 6.1 %multiply_convert_fusion.3 = bf16[128,4096]{0,1:T(8,128)(2,1)S(1)} fusion(bf16[128,4096]{0,1:T(8,128)(2,1)S(1)} %copy.85, bf16[3,4096]{0,1:T(8,128)(2,1)S(1)} %copy.84, f32[4096]{0:T(1024)S(1)} %bitcast.120, f32[4096]{0:T(1024)} %bitcast.121, f32[4096]{0:T(1024)S(1)} %bitcast.119, f32[4096]{0:T(1024)S(1)} %bitcast.118, f32[4096]{0:T(1024)} %param.19, ...), kind=kLoop, calls=%fused_computation.33 | loop fusion | flops 15204352 | bytes 2204032 | tf_op jit(solution)/shard_map/convert_element_type | solution.py:44
  29.6 1.8 convolution_bitcast_fusion
  31.5 1.3 copy.100
  32.8 18.0 %all-gather = f32[8,1,2,32]{3,2,1,0:T(2,128)S(1)} all-gather(f32[1,1,2,32]{3,2,1,0:T(2,128)S(1)} %copy-done.10), channel_id=2, replica_groups=mesh['groups'=2,'seq'=8,'heads'=2] {'seq'}, dimensions={0}, use_global_device_ids=true | all-gather | bytes 2304 | tf_op jit(solution)/shard_map/all_gather | solution.py:19
  51.1 3.3 fusion.1
  54.4 206.0 %all-gather.3.cloned.1.call-done = f32[8,2,32,128,64]{3,4,2,1,0:T(8,128)} async-done(((f32[1,2,32,128,64]{3,4,2,1,0:T(8,128)}), f32[8,2,32,128,64]{3,4,2,1,0:T(8,128)}) %all-gather.3.cloned.1.call-update) | async-done | bytes 16777232 | tf_op jit(solution)/shard_map/all_gather | solution.py:19
  260.4 82.5 %while.14 = (s32[]{:T(128)}, f32[2,32,128,64]{3,2,1,0:T(8,128)}, s32[]{:T(128)}, f32[8,2,32]{2,1,0:T(2,128)S(1)}, f32[8,2,32,128,64]{3,4,2,1,0:T(8,128)}, /*index=5*/s32[]{:T(128)}, s32[]{:T(128)}) while((s32[]{:T(128)}, f32[2,32,128,64]{3,2,1,0:T(8,128)}, s32[]{:T(128)}, f32[8,2,32]{2,1,0:T(2,128)S(1)}, ...), condition=%wide.region_8.9_spmd.clone, body=%wide.region_7.8_spmd.clone.sunk | while | flops 2097156 | bytes 14680937 | solution.py:29
  260.4 1.7 constant_dynamic-slice_fusion.2
  262.2 2.7 copy.113
  264.9 4.7 %fusion.47 = f32[2,32,128,64]{3,2,1,0:T(8,128)} fusion(f32[1,2,32,128,64]{4,3,2,1,0:T(8,128)} %copy.113, f32[2,32,128,64]{3,2,1,0:T(8,128)} %get-tuple-element.222, f32[2,32]{1,0:T(2,128)S(1)} %dynamic-slice_bitcast_fusion.2, pred[]{:T(512)S(6)} %compare.3, pred[]{:T(512)S(6)} %lt.22), kind=kLoop, calls=%fused_computation.1.clone.1 | loop fusion | flops 2097152 | bytes 6291714 | tf_op jit(solution)/shard_map/while/body/eval_jaxpr/jit(_where)/select_n | solution.py:27
  269.6 1.7 constant_dynamic-slice_fusion.2
  271.4 2.7 copy.113
  274.1 6.0 %fusion.47 = f32[2,32,128,64]{3,2,1,0:T(8,128)} fusion(f32[1,2,32,128,64]{4,3,2,1,0:T(8,128)} %copy.113, f32[2,32,128,64]{3,2,1,0:T(8,128)} %get-tuple-element.222, f32[2,32]{1,0:T(2,128)S(1)} %dynamic-slice_bitcast_fusion.2, pred[]{:T(512)S(6)} %compare.3, pred[]{:T(512)S(6)} %lt.22), kind=kLoop, calls=%fused_computation.1.clone.1 | loop fusion | flops 2097152 | bytes 6291714 | tf_op jit(solution)/shard_map/while/body/eval_jaxpr/jit(_where)/select_n | solution.py:27
  280.1 1.7 constant_dynamic-slice_fusion.2
  281.8 2.7 copy.113
  284.6 6.0 %fusion.47 = f32[2,32,128,64]{3,2,1,0:T(8,128)} fusion(f32[1,2,32,128,64]{4,3,2,1,0:T(8,128)} %copy.113, f32[2,32,128,64]{3,2,1,0:T(8,128)} %get-tuple-element.222, f32[2,32]{1,0:T(2,128)S(1)} %dynamic-slice_bitcast_fusion.2, pred[]{:T(512)S(6)} %compare.3, pred[]{:T(512)S(6)} %lt.22), kind=kLoop, calls=%fused_computation.1.clone.1 | loop fusion | flops 2097152 | bytes 6291714 | tf_op jit(solution)/shard_map/while/body/eval_jaxpr/jit(_where)/select_n | solution.py:27
  290.6 1.7 constant_dynamic-slice_fusion.2
  292.3 2.7 copy.113
  295.1 6.0 %fusion.47 = f32[2,32,128,64]{3,2,1,0:T(8,128)} fusion(f32[1,2,32,128,64]{4,3,2,1,0:T(8,128)} %copy.113, f32[2,32,128,64]{3,2,1,0:T(8,128)} %get-tuple-element.222, f32[2,32]{1,0:T(2,128)S(1)} %dynamic-slice_bitcast_fusion.2, pred[]{:T(512)S(6)} %compare.3, pred[]{:T(512)S(6)} %lt.22), kind=kLoop, calls=%fused_computation.1.clone.1 | loop fusion | flops 2097152 | bytes 6291714 | tf_op jit(solution)/shard_map/while/body/eval_jaxpr/jit(_where)/select_n | solution.py:27
  301.1 1.7 constant_dynamic-slice_fusion.2
  302.8 2.7 copy.113
  305.5 6.0 %fusion.47 = f32[2,32,128,64]{3,2,1,0:T(8,128)} fusion(f32[1,2,32,128,64]{4,3,2,1,0:T(8,128)} %copy.113, f32[2,32,128,64]{3,2,1,0:T(8,128)} %get-tuple-element.222, f32[2,32]{1,0:T(2,128)S(1)} %dynamic-slice_bitcast_fusion.2, pred[]{:T(512)S(6)} %compare.3, pred[]{:T(512)S(6)} %lt.22), kind=kLoop, calls=%fused_computation.1.clone.1 | loop fusion | flops 2097152 | bytes 6291714 | tf_op jit(solution)/shard_map/while/body/eval_jaxpr/jit(_where)/select_n | solution.py:27
  311.5 1.7 constant_dynamic-slice_fusion.2
  313.3 2.7 copy.113
  316.0 6.0 %fusion.47 = f32[2,32,128,64]{3,2,1,0:T(8,128)} fusion(f32[1,2,32,128,64]{4,3,2,1,0:T(8,128)} %copy.113, f32[2,32,128,64]{3,2,1,0:T(8,128)} %get-tuple-element.222, f32[2,32]{1,0:T(2,128)S(1)} %dynamic-slice_bitcast_fusion.2, pred[]{:T(512)S(6)} %compare.3, pred[]{:T(512)S(6)} %lt.22), kind=kLoop, calls=%fused_computation.1.clone.1 | loop fusion | flops 2097152 | bytes 6291714 | tf_op jit(solution)/shard_map/while/body/eval_jaxpr/jit(_where)/select_n | solution.py:27
  322.0 1.7 constant_dynamic-slice_fusion.2
  323.7 2.7 copy.113
  326.5 6.0 %fusion.47 = f32[2,32,128,64]{3,2,1,0:T(8,128)} fusion(f32[1,2,32,128,64]{4,3,2,1,0:T(8,128)} %copy.113, f32[2,32,128,64]{3,2,1,0:T(8,128)} %get-tuple-element.222, f32[2,32]{1,0:T(2,128)S(1)} %dynamic-slice_bitcast_fusion.2, pred[]{:T(512)S(6)} %compare.3, pred[]{:T(512)S(6)} %lt.22), kind=kLoop, calls=%fused_computation.1.clone.1 | loop fusion | flops 2097152 | bytes 6291714 | tf_op jit(solution)/shard_map/while/body/eval_jaxpr/jit(_where)/select_n | solution.py:27
  332.5 1.7 constant_dynamic-slice_fusion.2
  334.2 2.7 copy.113
  337.0 6.0 %fusion.47 = f32[2,32,128,64]{3,2,1,0:T(8,128)} fusion(f32[1,2,32,128,64]{4,3,2,1,0:T(8,128)} %copy.113, f32[2,32,128,64]{3,2,1,0:T(8,128)} %get-tuple-element.222, f32[2,32]{1,0:T(2,128)S(1)} %dynamic-slice_bitcast_fusion.2, pred[]{:T(512)S(6)} %compare.3, pred[]{:T(512)S(6)} %lt.22), kind=kLoop, calls=%fused_computation.1.clone.1 | loop fusion | flops 2097152 | bytes 6291714 | tf_op jit(solution)/shard_map/while/body/eval_jaxpr/jit(_where)/select_n | solution.py:27
  343.0 3.1 fusion.11
  346.6 0.7 copy-done
  347.3 0.8 bitcast_reduce_fusion
  348.1 0.9 fusion.10
  349.1 1.3 copy.101
  (61 shorter events, 4.8 us)
Async XLA Ops:
  6.5 15.6 %copy-start.3 = (bf16[128,2,256]{2,1,0:T(2,128)(2,1)S(1)}, bf16[128,2,256]{2,1,0:T(2,128)(2,1)}, u32[]{:S(2)}) copy-start(bf16[128,2,256]{2,1,0:T(2,128)(2,1)} %param.17) | copy-start | bytes 393220
  6.5 15.7 %copy-start.11 = (f32[2,256]{1,0:T(2,128)S(1)}, f32[2,256]{1,0:T(2,128)}, u32[]{:S(2)}) copy-start(f32[2,256]{1,0:T(2,128)} %param.21) | copy-start | bytes 6148
  6.5 253.9 %all-gather.3.cloned.1.call-start = ((), (), s32[]{:S(2)}) async-start(), calls=%async_computation | async-start | bytes 18874368 | tf_op jit(solution)/shard_map/all_gather | solution.py:19
  7.4 15.5 %collective-permute-start = (bf16[3,4096]{1,0:T(4,128)(2,1)S(1)}, bf16[3,4096]{1,0:T(4,128)(2,1)S(1)}, u32[]{:S(2)}, u32[]{:S(2)}) collective-permute-start(bf16[3,4096]{1,0:T(4,128)(2,1)S(1)} %slice.63), channel_id=1, source_target_pairs={{0,2},{2,4},{4,6},{6,8},{8,10},{10,12},{12,14},{1,3},{3,5},{5,7},{... | collective-permute-start | bytes 73736 | tf_op jit(solution)/shard_map/ppermute | solution.py:14
  9.6 12.6 %collective-permute-start.1 = (bf16[3,2,256]{0,2,1:T(8,128)(2,1)S(1)}, bf16[3,2,256]{0,2,1:T(8,128)(2,1)S(1)}, u32[]{:S(2)}, u32[]{:S(2)}) collective-permute-start(bf16[3,2,256]{0,2,1:T(8,128)(2,1)S(1)} %copy.90), channel_id=1, source_target_pairs={{0,2},{2,4},{4,6},{6,8},{8,10},{10,12},{12,14},{1,3},{3,5},{5,7},{... | collective-permute-start | bytes 9224 | tf_op jit(solution)/shard_map/ppermute | solution.py:14
  13.2 6.5 %copy-start.5 = (s32[128]{0:T(128)}, s32[128]{0:T(128)S(1)}, u32[]{:S(2)}) copy-start(s32[128]{0:T(128)S(1)} %get-tuple-element.158) | copy-start | bytes 1540
  19.6 2.7 copy-start.7
  19.6 2.7 copy-start.8
  19.6 2.7 copy-start.9
  29.5 1.9 copy-start.12
  29.5 2.0 copy-start.2
  31.3 1.5 copy-start.10
  31.3 19.5 %copy-start.6 = (s32[128]{0:T(128)S(1)}, s32[128]{0:T(128)}, u32[]{:S(2)}) copy-start(s32[128]{0:T(128)} %copy-done.5) | copy-start | bytes 1540
  343.0 3.1 copy-start.1
  346.0 1.2 copy-start
  347.3 0.8 copy-start.4
Sparse Core Ops, SparseCore 0:
  31.5 228.9 all-gather.2
where the time goes:
time: 363 us; the launch traced here: 357 us
  waiting for transfers between devices  206 us (57%)
  other arithmetic  62.4 us (17%)
  local copies, waits for them, and re-layouts  45.4 us (13%)
  blocking collectives  18 us (5%)
  between operations  14.3 us (4%)
  matrix products  8.34 us (2%)
    all_gather x1, waiting for transfers between devices, prefix_2(): everything = jax.tree.map(lambda part: lax.all_gather(part, axis), x)  206 us
    select_n x8, other arithmetic, step(): return jax.tree.map(lambda a, b: jnp.where(reached, a, b), new, before)  46.7 us
    dynamic_slice x16, local copies, waits for them, and re-layouts, step(): new = combine(before, jax.tree.map(lambda part: part[k], everything))  35.7 us
    all_gather x1, blocking collectives, prefix_2(): everything = jax.tree.map(lambda part: lax.all_gather(part, axis), x)  18 us
    dot_general x4, matrix products, contract(): return jnp.einsum(form, left, right, preferred_element_type=jnp.float32)  8.34 us
  transfers between devices with their start and end apart: 3, of which 1 were waited for; matrix products, arithmetic and copies ran while one was open for 5% of the time, Pallas kernels for 0%

commit v1 on v0

v1 whole, which is shorter than its diff:
```python
import functools

import jax
import jax.numpy as jnp
from jax import lax
from jax.experimental import pallas as pl
from jax.experimental.pallas import tpu as pltpu
from jax.sharding import PartitionSpec as P

HEAD_DIM = 64
STATE = 128
BLOCK = 128
TILE = 128
CHUNK = 256
EDGE = 16
LAG = 2
F32 = jnp.float32
BF16 = jnp.bfloat16
MESH = pl.DeviceIdType.MESH


def dot(a, b):
    return lax.dot_general(a, b, (((1,), (0,)), ((), ())), preferred_element_type=F32)


def silu(v):
    half = 0.5 * v
    return half + half * jnp.tanh(half)


def split(v):
    high = v.astype(BF16).astype(F32)
    return jnp.concatenate([high, v - high], axis=1)


def iota(shape, dim):
    return lax.broadcasted_iota(jnp.int32, shape, dim)


def spread(chunk, heads):
    per = CHUNK // HEAD_DIM
    row = iota((2 * heads, CHUNK), 0)
    col = iota((2 * heads, CHUNK), 1)
    head = jnp.where(row >= heads, row - heads, row)
    hit = head == chunk * per + lax.shift_right_logical(col, HEAD_DIM.bit_length() - 1)
    return jnp.where(hit, 1.0, 0.0).astype(BF16)


def conv_rows(values, weight, bias, flags, skip_rows):
    width = weight.shape[0]
    total = bias + values[skip_rows:] * weight[width - 1 : width]
    for d in range(1, width):
        moved = pltpu.roll(values, d, 0)[skip_rows:]
        total = total + moved * flags[d - 1] * weight[width - 1 - d : width - d]
    return silu(total).astype(BF16)


def kernel(
    peers,
    lengths,
    x_hbm,
    z_hbm,
    bc,
    wx,
    bx,
    wbc,
    bbc,
    dt,
    dtb,
    decay,
    skip,
    gain,
    out,
    xv,
    zv,
    xa,
    bca,
    xp,
    ent,
    flags,
    halo_x,
    halo_bc,
    mix,
    bt,
    grow,
    ggrow,
    vec,
    pvec,
    rows_x,
    prow,
    s_out,
    s_own,
    s_in,
    e_in,
    e_out,
    t_out,
    gated,
    sumsq,
    local_sem,
    halo_send,
    halo_recv,
    vec_send,
    vec_recv,
    s_send,
    s_recv,
    e_send,
    e_recv,
    t_send,
    t_recv,
):
    rows, chan = x_hbm.shape
    heads = dt.shape[1]
    groups = bc.shape[1] // (2 * STATE)
    chunks = chan // CHUNK
    pairs = chunks // 2
    pairs_per = pairs // groups
    me = lax.axis_index("seq")
    inner = lax.rem(me, 2)
    outer = lax.div(me, 2)
    last_outer = peers // 2 - 1
    partner = me + 1 - 2 * inner

    load_x = pltpu.make_async_copy(x_hbm, xv, local_sem.at[0])
    load_z = pltpu.make_async_copy(z_hbm, zv, local_sem.at[1])
    load_x.start()
    load_z.start()

    barrier = pltpu.get_barrier_semaphore()
    for step in (-2, -1, 1, 2):
        there = me + step

        @pl.when((there >= 0) & (there < peers))
        def _():
            pl.semaphore_signal(barrier, inc=1, device_id={"seq": there}, device_id_type=MESH)

    present = jnp.minimum(me, 2) + jnp.minimum(peers - 1 - me, 2)

    start = me * rows
    ends = []
    total = jnp.int32(0)
    for j in range(lengths.shape[0]):
        total = total + lengths[j]
        ends.append(total)

    def seg_of(pos):
        count = jnp.zeros_like(pos)
        for end in ends:
            count = count + jnp.where(pos >= end, 1, 0)
        return jnp.where(pos >= 0, count, -1)

    square = (rows, rows)
    pos = iota(square, 0) + start
    seg_t = seg_of(pos)
    for d in range(1, wx.shape[0]):
        flags[d - 1] = jnp.where(seg_of(pos - d) == seg_t, 1.0, 0.0)
    seg_s = seg_of(iota(square, 1) + start)
    seg_last = seg_of(jnp.zeros(square, jnp.int32) + (start + rows - 1))
    seg_prev = seg_of(jnp.zeros(square, jnp.int32) + (start - 1))
    mask = jnp.where((seg_t == seg_s) & (iota(square, 0) >= iota(square, 1)), 1.0, 0.0)
    to_end = jnp.where(seg_t == seg_last, 1.0, 0.0)
    live = jnp.where(seg_t == seg_prev, 1.0, 0.0)

    raw = dt[...].astype(F32) + dtb[...]
    rate = jnp.maximum(raw, 0.0) + jnp.log(1.0 + jnp.exp(-jnp.abs(raw)))
    a = -rate * decay[...]
    tri = jnp.where(iota(square, 0) >= iota(square, 1), 1.0, 0.0).astype(BF16)
    cum = jnp.zeros_like(a)
    rest = a
    for _ in range(3):
        part = rest.astype(BF16)
        cum = cum + dot(tri, part)
        rest = rest - part.astype(F32)
    grow[...] = split(jnp.exp(cum)).astype(BF16)
    ggrow[...] = split(jnp.exp(-cum) * rate).astype(BF16)
    whole = jnp.exp(cum[rows - 1 : rows, :])
    carry = live[rows - 1 : rows, :heads] * whole
    which = iota(vec.shape, 0)
    vec[...] = jnp.where(
        which == 0, split(carry), jnp.where(which == 1, split(whole), jnp.where(which == 2, split(skip[...]), 0.0))
    )

    pl.semaphore_wait(barrier, present)

    def halo_copies():
        there = jnp.minimum(me + 1, peers - 1)
        tail = pl.ds(rows - EDGE, EDGE)
        return [
            pltpu.make_async_remote_copy(
                x_hbm.at[tail], halo_x, halo_send.at[0], halo_recv.at[0], device_id={"seq": there}, device_id_type=MESH
            ),
            pltpu.make_async_remote_copy(
                bc.at[tail], halo_bc, halo_send.at[1], halo_recv.at[1], device_id={"seq": there}, device_id_type=MESH
            ),
        ]

    @pl.when(me < peers - 1)
    def _():
        for copy in halo_copies():
            copy.start()

    def vec_copy():
        return pltpu.make_async_remote_copy(
            vec, pvec, vec_send, vec_recv, device_id={"seq": partner}, device_id_type=MESH
        )

    vec_copy().start()

    for tile in range(bc.shape[1] // TILE):
        cols = slice(tile * TILE, (tile + 1) * TILE)
        bca[:, cols] = conv_rows(bc[:, cols].astype(F32), wbc[:, cols].astype(F32), bbc[:, cols], flags, 0)

    load_x.wait()

    def conv_tile(tile, _):
        cols = pl.ds(pl.multiple_of(tile * TILE, TILE), TILE)
        xa[:, cols] = conv_rows(xv[:, cols].astype(F32), wx[:, cols].astype(F32), bx[:, cols], flags, 0)
        return 0

    lax.fori_loop(0, chan // TILE, conv_tile, 0, unroll=2)

    @pl.when(me == 0)
    def _():
        halo_x[...] = jnp.zeros_like(halo_x)
        halo_bc[...] = jnp.zeros_like(halo_bc)

    @pl.when(me > 0)
    def _():
        for copy in halo_copies():
            copy.wait_recv()

    head_flags = [flags[d, :EDGE, :] for d in range(wx.shape[0] - 1)]
    for tile in range(bc.shape[1] // TILE):
        cols = slice(tile * TILE, (tile + 1) * TILE)
        values = jnp.concatenate([halo_bc[:, cols].astype(F32), bc[:EDGE, cols].astype(F32)], axis=0)
        bca[:EDGE, cols] = conv_rows(values, wbc[:, cols].astype(F32), bbc[:, cols], head_flags, EDGE)

    def conv_head(tile, _):
        cols = pl.ds(pl.multiple_of(tile * TILE, TILE), TILE)
        values = jnp.concatenate([halo_x[:, cols].astype(F32), xv[:EDGE, cols].astype(F32)], axis=0)
        some = [flags[d, :EDGE, :] for d in range(wx.shape[0] - 1)]
        xa[:EDGE, cols] = conv_rows(values, wx[:, cols].astype(F32), bx[:, cols], some, EDGE)
        return 0

    lax.fori_loop(0, chan // TILE, conv_head, 0, unroll=4)

    for g in range(groups):
        bmat = bca[:, g * STATE : (g + 1) * STATE].astype(F32)
        cmat = bca[:, (groups + g) * STATE : (groups + g + 1) * STATE]
        bmat_t = jnp.transpose(bmat)
        scores = dot(cmat, bmat_t.astype(BF16))
        mix[g, :, :rows] = (scores * mask).astype(BF16)
        mix[g, :, rows:] = (cmat.astype(F32) * live).astype(BF16)
        bt[g] = jnp.transpose(bmat * to_end).astype(BF16)

    def state_of(c):
        ex = spread(c, heads)
        cols = pl.ds(pl.multiple_of(c * CHUNK, CHUNK), CHUNK)
        scaled = (dot(ggrow[...], ex) * xa[:, cols].astype(F32)).astype(BF16)
        xp[c] = scaled
        rows_x[c] = dot(vec[...].astype(BF16), ex)
        return dot(bt[lax.div(c, chunks // groups)], scaled) * rows_x[c][1:2, :]

    def s_copy(j):
        return pltpu.make_async_remote_copy(
            s_out.at[j], s_in.at[j], s_send.at[j], s_recv.at[j], device_id={"seq": partner}, device_id_type=MESH
        )

    def e_copy(j):
        there = jnp.minimum(me + 2, peers - 1)
        return pltpu.make_async_remote_copy(
            e_out.at[j], e_in.at[j], e_send.at[j], e_recv.at[j], device_id={"seq": there}, device_id_type=MESH
        )

    def t_copy(j, c):
        return pltpu.make_async_remote_copy(
            t_out.at[j], ent.at[c], t_send.at[j], t_recv.at[j], device_id={"seq": partner}, device_id_type=MESH
        )

    def states(j, _):
        s_out[j] = state_of(2 * j + 1 - inner).astype(BF16)
        s_copy(j).start()
        s_own[j] = state_of(2 * j + inner)
        return 0

    lax.fori_loop(0, pairs, states, 0)

    @pl.when(outer == 0)
    def _():
        e_in[...] = jnp.zeros_like(e_in)

    vec_copy().wait_recv()
    pvec_b = pvec[...].astype(BF16)

    def partner_rows(j, _):
        prow[j] = dot(pvec_b, spread(2 * j + inner, heads))
        return 0

    lax.fori_loop(0, pairs, partner_rows, 0)
    sumsq[...] = jnp.zeros_like(sumsq)
    load_z.wait()

    def advance(j):
        c = 2 * j + inner
        s_copy(j).wait_recv()

        @pl.when(outer > 0)
        def _():
            e_copy(j).wait_recv()

        mine = s_own[j]
        other = s_in[j].astype(F32)
        c_mine = rows_x[c][0:1, :]
        c_other = prow[j][0:1, :]
        first = jnp.broadcast_to(inner, mine.shape) == 0
        row_first = jnp.broadcast_to(inner, c_mine.shape) == 0
        e = e_in[j].astype(F32)
        between = jnp.where(row_first, c_mine, c_other) * e + jnp.where(first, mine, other)
        after = jnp.where(row_first, c_other, c_mine) * between + jnp.where(first, other, mine)
        e_out[j] = after.astype(BF16)

        @pl.when(outer < last_outer)
        def _():
            e_copy(j).start()

        t_out[j] = jnp.where(first, between, e).astype(BF16)
        t_copy(j, c).start()
        ent[c] = jnp.where(first, e, between).astype(BF16)

    def finish_chunk(c):
        g = lax.div(c, chunks // groups)
        cols = pl.ds(pl.multiple_of(c * CHUNK, CHUNK), CHUNK)
        right = jnp.concatenate([xp[c], ent[c]], axis=0)
        y = dot(mix[g], right) * dot(grow[...], spread(c, heads))
        y = y + rows_x[c][2:3, :] * xa[:, cols].astype(F32)
        v = y.astype(BF16).astype(F32) * silu(zv[:, cols].astype(F32))
        gated[c] = v
        sumsq[g] = sumsq[g] + v * v

    def finish_pair(j):
        t_copy(j, 2 * j + 1 - inner).wait_recv()
        finish_chunk(2 * j)
        finish_chunk(2 * j + 1)

    def norm_group(g):
        size = chan // groups
        mean = jnp.sum(sumsq[g], axis=1, keepdims=True) * (1.0 / size)
        scale = lax.rsqrt(mean + 1e-05)

        def one(k, _):
            c = g * (chunks // groups) + k
            cols = pl.ds(pl.multiple_of(c * CHUNK, CHUNK), CHUNK)
            out[:, cols] = (gated[c] * scale * gain[:, cols]).astype(BF16)
            return 0

        lax.fori_loop(0, chunks // groups, one, 0, unroll=2)

    def lead(j, _):
        advance(j)
        return 0

    def steady(j, _):
        advance(j)
        finish_pair(j - LAG)

        @pl.when(lax.rem(j - LAG + 1, pairs_per) == 0)
        def _():
            norm_group(lax.div(j - LAG, pairs_per))

        return 0

    def tail(j, _):
        finish_pair(j)

        @pl.when(lax.rem(j + 1, pairs_per) == 0)
        def _():
            norm_group(lax.div(j, pairs_per))

        return 0

    lax.fori_loop(0, LAG, lead, 0)
    lax.fori_loop(LAG, pairs, steady, 0)
    lax.fori_loop(pairs - LAG, pairs, tail, 0)

    def drain(j, _):
        s_copy(j).wait_send()
        t_copy(j, 2 * j + inner).wait_send()

        @pl.when(outer < last_outer)
        def _():
            e_copy(j).wait_send()

        return 0

    lax.fori_loop(0, pairs, drain, 0)
    vec_copy().wait_send()

    @pl.when(me < peers - 1)
    def _():
        for copy in halo_copies():
            copy.wait_send()


def shards(peers, x_in, z_in, bc_in, wx, bx, wbc, bbc, dt_raw, dt_bias, decay, skip_d, gain, lengths):
    rows, chan = x_in.shape
    heads = dt_raw.shape[1]
    groups = bc_in.shape[2] // STATE
    width = wx.shape[0]
    chunks = chan // CHUNK
    pairs = chunks // 2
    bcw = 2 * groups * STATE
    vmem = pl.BlockSpec(memory_space=pltpu.VMEM)
    hbm = pl.BlockSpec(memory_space=pl.ANY)
    smem = pl.BlockSpec(memory_space=pltpu.SMEM)
    dma = pltpu.SemaphoreType.DMA
    return pl.pallas_call(
        functools.partial(kernel, peers),
        out_shape=jax.ShapeDtypeStruct((rows, chan), BF16),
        in_specs=[smem, hbm, hbm] + [vmem] * 10,
        out_specs=vmem,
        scratch_shapes=[
            pltpu.VMEM((rows, chan), BF16),
            pltpu.VMEM((rows, chan), BF16),
            pltpu.VMEM((rows, chan), BF16),
            pltpu.VMEM((rows, bcw), BF16),
            pltpu.VMEM((chunks, rows, CHUNK), BF16),
            pltpu.VMEM((chunks, STATE, CHUNK), BF16),
            pltpu.VMEM((width - 1, rows, TILE), F32),
            pltpu.VMEM((EDGE, chan), BF16),
            pltpu.VMEM((EDGE, bcw), BF16),
            pltpu.VMEM((groups, rows, rows + STATE), BF16),
            pltpu.VMEM((groups, STATE, rows), BF16),
            pltpu.VMEM((rows, 2 * heads), BF16),
            pltpu.VMEM((rows, 2 * heads), BF16),
            pltpu.VMEM((16, 2 * heads), F32),
            pltpu.VMEM((16, 2 * heads), F32),
            pltpu.VMEM((chunks, 16, CHUNK), F32),
            pltpu.VMEM((pairs, 16, CHUNK), F32),
            pltpu.VMEM((pairs, STATE, CHUNK), BF16),
            pltpu.VMEM((pairs, STATE, CHUNK), F32),
            pltpu.VMEM((pairs, STATE, CHUNK), BF16),
            pltpu.VMEM((pairs, STATE, CHUNK), BF16),
            pltpu.VMEM((pairs, STATE, CHUNK), BF16),
            pltpu.VMEM((pairs, STATE, CHUNK), BF16),
            pltpu.VMEM((chunks, rows, CHUNK), F32),
            pltpu.VMEM((groups, rows, CHUNK), F32),
            dma((2,)),
            dma((2,)),
            dma((2,)),
            dma,
            dma,
            dma((pairs,)),
            dma((pairs,)),
            dma((pairs,)),
            dma((pairs,)),
            dma((pairs,)),
            dma((pairs,)),
        ],
        compiler_params=pltpu.CompilerParams(
            collective_id=0, has_side_effects=True, vmem_limit_bytes=40 * 1024 * 1024
        ),
        name="mixer",
    )(
        lengths,
        x_in,
        z_in,
        bc_in.reshape(rows, bcw),
        wx,
        bx.reshape(1, chan),
        wbc.reshape(width, bcw),
        bbc.reshape(1, bcw),
        dt_raw,
        dt_bias.reshape(1, heads),
        decay.reshape(1, heads),
        skip_d.reshape(1, heads),
        gain.reshape(1, chan),
    )


def solution(mesh):
    return jax.shard_map(
        functools.partial(shards, mesh.shape["seq"]),
        mesh=mesh,
        in_specs=(
            P(("groups", "seq"), "heads"),
            P(("groups", "seq"), "heads"),
            P(("groups", "seq"), None, "heads"),
            P(None, "heads"),
            P("heads"),
            P(None, None, "heads"),
            P(None, "heads"),
            P(("groups", "seq"), "heads"),
            P("heads"),
            P("heads"),
            P("heads"),
            P("heads"),
            P("groups"),
        ),
        out_specs=P(("groups", "seq"), "heads"),
        check_vma=False,
    )
```

time: 363 us -> 48.4 us (0.13)
  the two profiles are of different devices: /device:TPU:30 before, /device:TPU:26 now
where the time goes in v1:
time: 48.4 us; the launch traced here: 48.1 us
  Pallas kernels  42.1 us (87%)
  local copies, waits for them, and re-layouts  5.85 us (12%)
    pallas_call x1, Pallas kernels, shards(): pl.pallas_call(functools.partial(kernel, peers), out_shape=jax.ShapeDtype...  42.1 us
    unnamed x27, local copies, waits for them, and re-layouts  5.85 us

profile of v1, /device:TPU:26, one launch (start us, length us, event | category | flops | bytes accessed | tf_op | source)
XLA Modules:
  0.0 48.1 jit_solution(5067892680685388578)
XLA Ops:
  0.0 0.0 copy-start.9
  0.0 0.0 copy-start.10
  0.0 0.7 %copy.17 = f32[1,1,2,256]{3,1,2,0:T(1,128)S(1)} copy(f32[1,1,2,256]{3,2,1,0:T(2,128)} %bitcast.22) | data formatting | bytes 4096
  0.7 0.0 copy-done.10
  0.7 0.0 copy-done.9
  0.7 0.1 copy.14.dt
  0.9 0.0 copy-start.2
  0.9 0.0 copy-start.3
  0.9 0.0 copy-start.4
  0.9 0.0 copy-start.8
  0.9 0.9 %copy.15 = bf16[16,8,2,256]{3,1,2,0:T(8,128)(2,1)S(1)} copy(bf16[16,8,2,256]{3,2,1,0:T(2,128)(2,1)} %bitcast.20) | data formatting | bytes 262144
  1.8 0.0 copy-start.5
  1.9 0.0 copy-start.6
  1.9 0.0 copy-start.7
  1.9 0.0 copy-done.2
  1.9 0.0 copy-done.3
  1.9 0.0 copy-done.4
  1.9 0.0 copy-done.8
  1.9 0.6 %copy-done.5 = s32[8]{0:T(128)S(1)} copy-done((s32[8]{0:T(128)S(1)}, s32[8]{0:T(128)}, u32[]{:S(2)}) %copy-start.5) | copy-done | bytes 56
  2.5 0.0 copy-done.6
  2.5 0.0 copy-done.7
  2.5 0.0 copy-start
  2.5 1.2 %copy-done = bf16[128,4096]{1,0:T(8,128)(2,1)S(1)} copy-done((bf16[128,4096]{1,0:T(8,128)(2,1)S(1)}, bf16[128,4096]{1,0:T(8,128)(2,1)}, u32[]{:S(2)}) %copy-start) | copy-done | bytes 1048600
  3.8 0.0 copy-start.1
  3.8 1.2 %copy-done.1 = bf16[128,4096]{1,0:T(8,128)(2,1)S(1)} copy-done((bf16[128,4096]{1,0:T(8,128)(2,1)S(1)}, bf16[128,4096]{1,0:T(8,128)(2,1)}, u32[]{:S(2)}) %copy-start.1) | copy-done | bytes 1048600
  5.0 42.1 %mixer.1 = bf16[128,4096]{1,0:T(8,128)(2,1)S(1)} custom-call(s32[8]{0:T(128)S(1)} %copy-done.5, bf16[128,4096]{1,0:T(8,128)(2,1)S(1)} %copy-done, bf16[128,4096]{1,0:T(8,128)(2,1)S(1)} %copy-done.1, bf16[128,512]{1,0:T(8,128)(2,1)S(1)} %bitcast.12, bf16[4,4096]{1,0:T(4,128)(2,1)S(1)} %copy-done.2, f32[1,4096]{1,0:T(1,128)S(1)} %bitcast.13, ...), custom_call_target="tpu_custom_call" | custom-call | tf_op jit(solution)/shard_map/mixer/pallas_call | solution.py:415
  47.1 1.0 %copy.19 = bf16[128,4096]{1,0:T(8,128)(2,1)} copy(bf16[128,4096]{1,0:T(8,128)(2,1)S(1)} %mixer.1) | data formatting | bytes 2097152
  (1 shorter events, 0.0 us)
Async XLA Ops:
  0.0 0.7 %copy-start.9 = (bf16[128,64]{0,1:T(8,128)(2,1)S(1)}, bf16[128,64]{0,1:T(8,128)(2,1)}, u32[]{:S(2)}) copy-start(bf16[128,64]{0,1:T(8,128)(2,1)} %param.20) | copy-start | bytes 49156
  0.0 0.7 %copy-start.10 = (bf16[4,2,256]{2,1,0:T(2,128)(2,1)S(1)}, bf16[4,2,256]{2,1,0:T(2,128)(2,1)}, u32[]{:S(2)}) copy-start(bf16[4,2,256]{2,1,0:T(2,128)(2,1)} %param.18) | copy-start | bytes 12292
  0.9 1.0 %copy-start.2 = (bf16[4,4096]{1,0:T(4,128)(2,1)S(1)}, bf16[4,4096]{1,0:T(4,128)(2,1)}, u32[]{:S(2)}) copy-start(bf16[4,4096]{1,0:T(4,128)(2,1)} %wx.1) | copy-start | bytes 98308
  0.9 1.0 %copy-start.3 = (f32[4096]{0:T(1024)S(1)}, f32[4096]{0:T(1024)}, u32[]{:S(2)}) copy-start(f32[4096]{0:T(1024)} %param.17) | copy-start | bytes 49156
  0.9 1.0 %copy-start.4 = (f32[4096]{0:T(1024)S(1)}, f32[4096]{0:T(1024)}, u32[]{:S(2)}) copy-start(f32[4096]{0:T(1024)} %param.24) | copy-start | bytes 49156
  0.9 1.0 %copy-start.8 = (f32[64]{0:T(128)S(1)}, f32[64]{0:T(128)}, u32[]{:S(2)}) copy-start(f32[64]{0:T(128)} %param.23) | copy-start | bytes 772
  1.8 0.7 %copy-start.5 = (s32[8]{0:T(128)S(1)}, s32[8]{0:T(128)}, u32[]{:S(2)}) copy-start(s32[8]{0:T(128)} %lengths.1) | copy-start | bytes 100
  1.9 0.7 %copy-start.6 = (f32[64]{0:T(128)S(1)}, f32[64]{0:T(128)}, u32[]{:S(2)}) copy-start(f32[64]{0:T(128)} %param.21) | copy-start | bytes 772
  1.9 0.7 %copy-start.7 = (f32[64]{0:T(128)S(1)}, f32[64]{0:T(128)}, u32[]{:S(2)}) copy-start(f32[64]{0:T(128)} %param.22) | copy-start | bytes 772
  2.5 1.2 %copy-start = (bf16[128,4096]{1,0:T(8,128)(2,1)S(1)}, bf16[128,4096]{1,0:T(8,128)(2,1)}, u32[]{:S(2)}) copy-start(bf16[128,4096]{1,0:T(8,128)(2,1)} %x_hbm.1) | copy-start | bytes 3145732
  3.8 1.2 %copy-start.1 = (bf16[128,4096]{1,0:T(8,128)(2,1)S(1)}, bf16[128,4096]{1,0:T(8,128)(2,1)}, u32[]{:S(2)}) copy-start(bf16[128,4096]{1,0:T(8,128)(2,1)} %z_hbm.1) | copy-start | bytes 3145732

commit v2 on v1

--- a/solution.py
+++ b/solution.py
@@ -14,6 +14,8 @@
 CHUNK = 256
 EDGE = 16
 LAG = 2
+EARLY = 3
+FOLD = 4
 F32 = jnp.float32
 BF16 = jnp.bfloat16
 MESH = pl.DeviceIdType.MESH
@@ -80,6 +82,9 @@
     flags,
     halo_x,
     halo_bc,
+    fold_out,
+    fold_in,
+    spreads,
     mix,
     bt,
     grow,
@@ -87,7 +92,6 @@
     vec,
     pvec,
     rows_x,
-    prow,
     s_out,
     s_own,
     s_in,
@@ -179,6 +183,16 @@
         which == 0, split(carry), jnp.where(which == 1, split(whole), jnp.where(which == 2, split(skip[...]), 0.0))
     )
 
+    load_x.wait()
+    run = chan // FOLD
+    quarter = lax.shift_right_logical(iota((EDGE, run), 0), 2)
+    folded = jnp.zeros((EDGE, run), F32)
+    for m in range(FOLD):
+        piece = xv[rows - EDGE :, m * run : (m + 1) * run].astype(F32)
+        moved = pltpu.roll(piece, 4 * m + 4, 0) if m < FOLD - 1 else piece
+        folded = jnp.where(quarter == m, moved, folded)
+    fold_out[...] = folded.astype(BF16)
+
     pl.semaphore_wait(barrier, present)
 
     def halo_copies():
@@ -186,7 +200,7 @@
         tail = pl.ds(rows - EDGE, EDGE)
         return [
             pltpu.make_async_remote_copy(
-                x_hbm.at[tail], halo_x, halo_send.at[0], halo_recv.at[0], device_id={"seq": there}, device_id_type=MESH
+                fold_out, fold_in, halo_send.at[0], halo_recv.at[0], device_id={"seq": there}, device_id_type=MESH
             ),
             pltpu.make_async_remote_copy(
                 bc.at[tail], halo_bc, halo_send.at[1], halo_recv.at[1], device_id={"seq": there}, device_id_type=MESH
@@ -205,22 +219,34 @@
 
     vec_copy().start()
 
-    for tile in range(bc.shape[1] // TILE):
+    bcols = groups * STATE
+
+    def bc_params(tile):
+        cols = slice((tile % groups) * TILE, (tile % groups + 1) * TILE)
+        which = tile // groups
+        return wbc[:, tile * TILE : (tile + 1) * TILE].astype(F32), bbc[which : which + 1, cols]
+
+    bc_tiles = 2 * bcols // TILE
+    for tile in range(bc_tiles):
         cols = slice(tile * TILE, (tile + 1) * TILE)
-        bca[:, cols] = conv_rows(bc[:, cols].astype(F32), wbc[:, cols].astype(F32), bbc[:, cols], flags, 0)
-
-    load_x.wait()
+        weight, bias = bc_params(tile)
+        bca[:, cols] = conv_rows(bc[:, cols].astype(F32), weight, bias, flags, 0)
+
+    def x_params(cols):
+        return wx[:, cols].astype(F32), bx[:, cols]
 
     def conv_tile(tile, _):
         cols = pl.ds(pl.multiple_of(tile * TILE, TILE), TILE)
-        xa[:, cols] = conv_rows(xv[:, cols].astype(F32), wx[:, cols].astype(F32), bx[:, cols], flags, 0)
-        return 0
-
-    lax.fori_loop(0, chan // TILE, conv_tile, 0, unroll=2)
+        weight, bias = x_params(cols)
+        xa[:, cols] = conv_rows(xv[:, cols].astype(F32), weight, bias, flags, 0)
+        return 0
+
+    early_tiles = EARLY * 2 * CHUNK // TILE
+    lax.fori_loop(0, early_tiles, conv_tile, 0, unroll=2)
 
     @pl.when(me == 0)
     def _():
-        halo_x[...] = jnp.zeros_like(halo_x)
+        fold_in[...] = jnp.zeros_like(fold_in)
         halo_bc[...] = jnp.zeros_like(halo_bc)
 
     @pl.when(me > 0)
@@ -228,20 +254,34 @@
         for copy in halo_copies():
             copy.wait_recv()
 
+    for m in range(FOLD):
+        piece = fold_in[...].astype(F32)
+        moved = pltpu.roll(piece, EDGE - 4 * m - 4, 0) if m < FOLD - 1 else piece
+        halo_x[:, m * run : (m + 1) * run] = moved.astype(BF16)
+
     head_flags = [flags[d, :EDGE, :] for d in range(wx.shape[0] - 1)]
-    for tile in range(bc.shape[1] // TILE):
+    for tile in range(bc_tiles):
         cols = slice(tile * TILE, (tile + 1) * TILE)
+        weight, bias = bc_params(tile)
         values = jnp.concatenate([halo_bc[:, cols].astype(F32), bc[:EDGE, cols].astype(F32)], axis=0)
-        bca[:EDGE, cols] = conv_rows(values, wbc[:, cols].astype(F32), bbc[:, cols], head_flags, EDGE)
+        bca[:EDGE, cols] = conv_rows(values, weight, bias, head_flags, EDGE)
 
     def conv_head(tile, _):
         cols = pl.ds(pl.multiple_of(tile * TILE, TILE), TILE)
+        weight, bias = x_params(cols)
         values = jnp.concatenate([halo_x[:, cols].astype(F32), xv[:EDGE, cols].astype(F32)], axis=0)
         some = [flags[d, :EDGE, :] for d in range(wx.shape[0] - 1)]
-        xa[:EDGE, cols] = conv_rows(values, wx[:, cols].astype(F32), bx[:, cols], some, EDGE)
-        return 0
-
-    lax.fori_loop(0, chan // TILE, conv_head, 0, unroll=4)
+        xa[:EDGE, cols] = conv_rows(values, weight, bias, some, EDGE)
+        return 0
+
+    lax.fori_loop(0, early_tiles, conv_head, 0, unroll=2)
+
+    def conv_whole(tile, _):
+        cols = pl.ds(pl.multiple_of(tile * TILE, TILE), TILE)
+        weight, bias = x_params(cols)
+        values = jnp.concatenate([halo_x[:, cols].astype(F32), xv[:, cols].astype(F32)], axis=0)
+        xa[:, cols] = conv_rows(values, weight, bias, flags, EDGE)
+        return 0
 
     for g in range(groups):
         bmat = bca[:, g * STATE : (g + 1) * STATE].astype(F32)
@@ -254,6 +294,7 @@
 
     def state_of(c):
         ex = spread(c, heads)
+        spreads[c] = ex
         cols = pl.ds(pl.multiple_of(c * CHUNK, CHUNK), CHUNK)
         scaled = (dot(ggrow[...], ex) * xa[:, cols].astype(F32)).astype(BF16)
         xp[c] = scaled
@@ -276,29 +317,6 @@
             t_out.at[j], ent.at[c], t_send.at[j], t_recv.at[j], device_id={"seq": partner}, device_id_type=MESH
         )
 
-    def states(j, _):
-        s_out[j] = state_of(2 * j + 1 - inner).astype(BF16)
-        s_copy(j).start()
-        s_own[j] = state_of(2 * j + inner)
-        return 0
-
-    lax.fori_loop(0, pairs, states, 0)
-
-    @pl.when(outer == 0)
-    def _():
-        e_in[...] = jnp.zeros_like(e_in)
-
-    vec_copy().wait_recv()
-    pvec_b = pvec[...].astype(BF16)
-
-    def partner_rows(j, _):
-        prow[j] = dot(pvec_b, spread(2 * j + inner, heads))
-        return 0
-
-    lax.fori_loop(0, pairs, partner_rows, 0)
-    sumsq[...] = jnp.zeros_like(sumsq)
-    load_z.wait()
-
     def advance(j):
         c = 2 * j + inner
         s_copy(j).wait_recv()
@@ -310,7 +328,7 @@
         mine = s_own[j]
         other = s_in[j].astype(F32)
         c_mine = rows_x[c][0:1, :]
-        c_other = prow[j][0:1, :]
+        c_other = dot(pvec[...].astype(BF16), spreads[c])[0:1, :]
         first = jnp.broadcast_to(inner, mine.shape) == 0
         row_first = jnp.broadcast_to(inner, c_mine.shape) == 0
         e = e_in[j].astype(F32)
@@ -326,11 +344,39 @@
         t_copy(j, c).start()
         ent[c] = jnp.where(first, e, between).astype(BF16)
 
+    @pl.when(outer == 0)
+    def _():
+        e_in[...] = jnp.zeros_like(e_in)
+
+    vec_copy().wait_recv()
+    sumsq[...] = jnp.zeros_like(sumsq)
+    ahead = jnp.where(outer == 0, pairs - LAG, 0)
+
+    def states(j, _):
+        @pl.when(j >= EARLY)
+        def _():
+            per = 2 * CHUNK // TILE
+            for k in range(per):
+                conv_whole(j * per + k, 0)
+
+        s_out[j] = state_of(2 * j + 1 - inner).astype(BF16)
+        s_copy(j).start()
+        s_own[j] = state_of(2 * j + inner)
+
+        @pl.when((outer == 0) & (j >= LAG))
+        def _():
+            advance(j - LAG)
+
+        return 0
+
+    lax.fori_loop(0, pairs, states, 0)
+    load_z.wait()
+
     def finish_chunk(c):
         g = lax.div(c, chunks // groups)
         cols = pl.ds(pl.multiple_of(c * CHUNK, CHUNK), CHUNK)
         right = jnp.concatenate([xp[c], ent[c]], axis=0)
-        y = dot(mix[g], right) * dot(grow[...], spread(c, heads))
+        y = dot(mix[g], right) * dot(grow[...], spreads[c])
         y = y + rows_x[c][2:3, :] * xa[:, cols].astype(F32)
         v = y.astype(BF16).astype(F32) * silu(zv[:, cols].astype(F32))
         gated[c] = v
@@ -355,11 +401,17 @@
         lax.fori_loop(0, chunks // groups, one, 0, unroll=2)
 
     def lead(j, _):
-        advance(j)
+        @pl.when(j >= ahead)
+        def _():
+            advance(j)
+
         return 0
 
     def steady(j, _):
-        advance(j)
+        @pl.when(j >= ahead)
+        def _():
+            advance(j)
+
         finish_pair(j - LAG)
 
         @pl.when(lax.rem(j - LAG + 1, pairs_per) == 0)
@@ -427,6 +479,9 @@
             pltpu.VMEM((width - 1, rows, TILE), F32),
             pltpu.VMEM((EDGE, chan), BF16),
             pltpu.VMEM((EDGE, bcw), BF16),
+            pltpu.VMEM((EDGE, chan // FOLD), BF16),
+            pltpu.VMEM((EDGE, chan // FOLD), BF16),
+            pltpu.VMEM((chunks, 2 * heads, CHUNK), BF16),
             pltpu.VMEM((groups, rows, rows + STATE), BF16),
             pltpu.VMEM((groups, STATE, rows), BF16),
             pltpu.VMEM((rows, 2 * heads), BF16),
@@ -434,7 +489,6 @@
             pltpu.VMEM((16, 2 * heads), F32),
             pltpu.VMEM((16, 2 * heads), F32),
             pltpu.VMEM((chunks, 16, CHUNK), F32),
-            pltpu.VMEM((pairs, 16, CHUNK), F32),
             pltpu.VMEM((pairs, STATE, CHUNK), BF16),
             pltpu.VMEM((pairs, STATE, CHUNK), F32),
             pltpu.VMEM((pairs, STATE, CHUNK), BF16),
@@ -456,7 +510,7 @@
             dma((pairs,)),
         ],
         compiler_params=pltpu.CompilerParams(
-            collective_id=0, has_side_effects=True, vmem_limit_bytes=40 * 1024 * 1024
+            collective_id=0, has_side_effects=True, vmem_limit_bytes=63 * 1024 * 1024
         ),
         name="mixer",
     )(
@@ -467,7 +521,7 @@
         wx,
         bx.reshape(1, chan),
         wbc.reshape(width, bcw),
-        bbc.reshape(1, bcw),
+        bbc,
         dt_raw,
         dt_bias.reshape(1, heads),
         decay.reshape(1, heads),

time: 48.4 us -> 47.1 us (0.973)
  the two profiles are of different devices: /device:TPU:26 before, /device:TPU:30 now
where the time goes in v2:
time: 47.1 us; the launch traced here: 46.7 us
  Pallas kernels  40.8 us (87%)
  local copies, waits for them, and re-layouts  5.88 us (12%)
    pallas_call x1, Pallas kernels, shards(): pl.pallas_call(functools.partial(kernel, peers), out_shape=jax.ShapeDtype...  40.8 us
    unnamed x6, local copies, waits for them, and re-layouts  5.88 us

profile of v2, /device:TPU:30, one launch (start us, length us, event | category | flops | bytes accessed | tf_op | source)
XLA Modules:
  0.0 46.7 jit_solution(13206225872601630886)
XLA Ops:
  0.0 0.0 copy-start
  0.0 1.3 %copy.16 = bf16[1,4,2,256]{3,1,2,0:T(4,128)(2,1)} copy(bf16[1,4,2,256]{3,2,1,0:T(2,128)(2,1)} %bitcast.14) | data formatting | bytes 8192
  1.3 0.0 copy-done
  1.3 0.7 %copy.14.dt = bf16[128,64]{1,0:T(8,128)(2,1)} copy(bf16[128,64]{0,1:T(8,128)(2,1)S(1)} %copy-done) | data formatting | bytes 32768 | tf_op args[7]
  2.0 1.6 %copy.15 = bf16[16,8,2,256]{3,1,2,0:T(8,128)(2,1)} copy(bf16[16,8,2,256]{3,2,1,0:T(2,128)(2,1)} %bitcast.10) | data formatting | bytes 262144
  3.6 40.8 %mixer.1 = bf16[128,4096]{1,0:T(8,128)(2,1)} custom-call(s32[8]{0:T(128)} %lengths.1, bf16[128,4096]{1,0:T(8,128)(2,1)} %x_hbm.1, bf16[128,4096]{1,0:T(8,128)(2,1)} %z_hbm.1, bf16[128,512]{1,0:T(8,128)(2,1)} %bitcast.9, bf16[4,4096]{1,0:T(4,128)(2,1)} %wx.1, f32[1,4096]{1,0:T(1,128)} %bitcast.11, bf16[4,512]{1,0:T(4,128)(2,1)} %bitcast.13, f32[2,256]{1,0:T(2,128)} %bbc.1, ...), custom_call_target="tpu_custom_call" | custom-call | tf_op jit(solution)/shard_map/mixer/pallas_call | solution.py:467
  44.4 2.3 %copy.18 = bf16[128,4096]{1,0:T(8,128)(2,1)} copy(bf16[128,4096]{1,0:T(8,128)(2,1)} %mixer.1) | data formatting | bytes 2097152
Async XLA Ops:
  0.0 1.3 %copy-start = (bf16[128,64]{0,1:T(8,128)(2,1)S(1)}, bf16[128,64]{0,1:T(8,128)(2,1)}, u32[]{:S(2)}) copy-start(bf16[128,64]{0,1:T(8,128)(2,1)} %param.20) | copy-start | bytes 49156

commit v3 on v2

--- a/solution.py
+++ b/solution.py
@@ -317,6 +317,9 @@
             t_out.at[j], ent.at[c], t_send.at[j], t_recv.at[j], device_id={"seq": partner}, device_id_type=MESH
         )
 
+    hold = jnp.maximum(pairs - 1 - 2 * outer, 0)
+    behind = jnp.minimum(hold + LAG, pairs)
+
     def advance(j):
         c = 2 * j + inner
         s_copy(j).wait_recv()
@@ -341,7 +344,19 @@
             e_copy(j).start()
 
         t_out[j] = jnp.where(first, between, e).astype(BF16)
-        t_copy(j, c).start()
+
+        @pl.when(j == hold)
+        def _():
+            def release(k, _):
+                t_copy(k, 2 * k + inner).start()
+                return 0
+
+            lax.fori_loop(0, hold + 1, release, 0)
+
+        @pl.when(j > hold)
+        def _():
+            t_copy(j, c).start()
+
         ent[c] = jnp.where(first, e, between).astype(BF16)
 
     @pl.when(outer == 0)
@@ -400,38 +415,25 @@
 
         lax.fori_loop(0, chunks // groups, one, 0, unroll=2)
 
-    def lead(j, _):
-        @pl.when(j >= ahead)
+    def finish_and_norm(j):
+        finish_pair(j)
+
+        @pl.when(lax.rem(j + 1, pairs_per) == 0)
+        def _():
+            norm_group(lax.div(j, pairs_per))
+
+    def steady(j, _):
+        @pl.when((j >= ahead) & (j < pairs))
         def _():
             advance(j)
 
+        @pl.when(j >= behind)
+        def _():
+            finish_and_norm(j - behind)
+
         return 0
 
-    def steady(j, _):
-        @pl.when(j >= ahead)
-        def _():
-            advance(j)
-
-        finish_pair(j - LAG)
-
-        @pl.when(lax.rem(j - LAG + 1, pairs_per) == 0)
-        def _():
-            norm_group(lax.div(j - LAG, pairs_per))
-
-        return 0
-
-    def tail(j, _):
-        finish_pair(j)
-
-        @pl.when(lax.rem(j + 1, pairs_per) == 0)
-        def _():
-            norm_group(lax.div(j, pairs_per))
-
-        return 0
-
-    lax.fori_loop(0, LAG, lead, 0)
-    lax.fori_loop(LAG, pairs, steady, 0)
-    lax.fori_loop(pairs - LAG, pairs, tail, 0)
+    lax.fori_loop(0, pairs + behind, steady, 0)
 
     def drain(j, _):
         s_copy(j).wait_send()
@@ -461,7 +463,7 @@
     pairs = chunks // 2
     bcw = 2 * groups * STATE
     vmem = pl.BlockSpec(memory_space=pltpu.VMEM)
-    hbm = pl.BlockSpec(memory_space=pl.ANY)
+    hbm = pl.BlockSpec(memory_space=pltpu.HBM)
     smem = pl.BlockSpec(memory_space=pltpu.SMEM)
     dma = pltpu.SemaphoreType.DMA
     return pl.pallas_call(
@@ -510,7 +512,7 @@
             dma((pairs,)),
         ],
         compiler_params=pltpu.CompilerParams(
-            collective_id=0, has_side_effects=True, vmem_limit_bytes=63 * 1024 * 1024
+            collective_id=0, has_side_effects=True, vmem_limit_bytes=52 * 1024 * 1024
         ),
         name="mixer",
     )(

time: 47.1 us -> 36.8 us (0.78)
  Pallas kernels: 40.8 us -> 33 us
  local copies, waits for them, and re-layouts: 5.88 us -> 3.4 us
    pallas_call x1, Pallas kernels: 40.8 us -> 33 us  [shards(): pl.pallas_call(functools.partial(kernel, peers), out_shape=jax.ShapeDtype...]
    unnamed x6 -> x22, local copies, waits for them, and re-layouts: 5.88 us -> 3.4 us
where the time goes in v3:
time: 36.8 us; the launch traced here: 36.6 us
  Pallas kernels  33 us (90%)
  local copies, waits for them, and re-layouts  3.4 us (9%)
    pallas_call x1, Pallas kernels, shards(): pl.pallas_call(functools.partial(kernel, peers), out_shape=jax.ShapeDtype...  33 us
    unnamed x22, local copies, waits for them, and re-layouts  3.4 us

profile of v3, /device:TPU:30, one launch (start us, length us, event | category | flops | bytes accessed | tf_op | source)
XLA Modules:
  0.0 36.6 jit_solution(17775550799070695579)
XLA Ops:
  0.0 0.0 copy-start.8
  0.0 0.7 %copy.16 = bf16[1,4,2,256]{3,1,2,0:T(4,128)(2,1)S(1)} copy(bf16[1,4,2,256]{3,2,1,0:T(2,128)(2,1)} %bitcast.17) | data formatting | bytes 8192
  0.7 0.0 copy-done.8
  0.7 0.1 copy.14.dt
  0.8 0.0 copy-start
  0.8 0.0 copy-start.1
  0.9 0.0 copy-start.2
  0.9 0.0 copy-start.3
  0.9 0.0 copy-start.7
  0.9 0.9 %copy.15 = bf16[16,8,2,256]{3,1,2,0:T(8,128)(2,1)S(1)} copy(bf16[16,8,2,256]{3,2,1,0:T(2,128)(2,1)} %bitcast.16) | data formatting | bytes 262144
  1.8 0.0 copy-start.4
  1.9 0.0 copy-start.5
  1.9 0.0 copy-start.6
  1.9 0.0 copy-done
  1.9 0.0 copy-done.1
  1.9 0.0 copy-done.2
  1.9 0.0 copy-done.3
  1.9 0.0 copy-done.7
  1.9 0.6 %copy-done.4 = s32[8]{0:T(128)S(1)} copy-done((s32[8]{0:T(128)S(1)}, s32[8]{0:T(128)}, u32[]{:S(2)}) %copy-start.4) | copy-done | bytes 56
  2.5 0.0 copy-done.5
  2.5 0.0 copy-done.6
  2.5 33.0 %mixer.1 = bf16[128,4096]{1,0:T(8,128)(2,1)S(1)} custom-call(s32[8]{0:T(128)S(1)} %copy-done.4, bf16[128,4096]{1,0:T(8,128)(2,1)} %x_hbm.1, bf16[128,4096]{1,0:T(8,128)(2,1)} %z_hbm.1, bf16[128,512]{1,0:T(8,128)(2,1)S(1)} %bitcast.9, bf16[4,4096]{1,0:T(4,128)(2,1)S(1)} %copy-done, f32[1,4096]{1,0:T(1,128)S(1)} %bitcast.10, bf16[4,512]{1,0:T(4,128)(2,1)S(1)} %bitcast.12, ...), custom_call_target="tpu_custom_call" | custom-call | tf_op jit(solution)/shard_map/mixer/pallas_call | solution.py:469
  35.6 1.0 %copy.18 = bf16[128,4096]{1,0:T(8,128)(2,1)} copy(bf16[128,4096]{1,0:T(8,128)(2,1)S(1)} %mixer.1) | data formatting | bytes 2097152
Async XLA Ops:
  0.0 0.7 %copy-start.8 = (bf16[128,64]{0,1:T(8,128)(2,1)S(1)}, bf16[128,64]{0,1:T(8,128)(2,1)}, u32[]{:S(2)}) copy-start(bf16[128,64]{0,1:T(8,128)(2,1)} %param.20) | copy-start | bytes 49156
  0.8 1.1 %copy-start = (bf16[4,4096]{1,0:T(4,128)(2,1)S(1)}, bf16[4,4096]{1,0:T(4,128)(2,1)}, u32[]{:S(2)}) copy-start(bf16[4,4096]{1,0:T(4,128)(2,1)} %wx.1) | copy-start | bytes 98308
  0.8 1.0 %copy-start.1 = (f32[4096]{0:T(1024)S(1)}, f32[4096]{0:T(1024)}, u32[]{:S(2)}) copy-start(f32[4096]{0:T(1024)} %param.17) | copy-start | bytes 49156
  0.9 1.0 %copy-start.2 = (f32[4096]{0:T(1024)S(1)}, f32[4096]{0:T(1024)}, u32[]{:S(2)}) copy-start(f32[4096]{0:T(1024)} %param.24) | copy-start | bytes 49156
  0.9 1.0 %copy-start.3 = (f32[2,256]{1,0:T(2,128)S(1)}, f32[2,256]{1,0:T(2,128)}, u32[]{:S(2)}) copy-start(f32[2,256]{1,0:T(2,128)} %bbc.1) | copy-start | bytes 6148
  0.9 1.0 %copy-start.7 = (f32[64]{0:T(128)S(1)}, f32[64]{0:T(128)}, u32[]{:S(2)}) copy-start(f32[64]{0:T(128)} %param.23) | copy-start | bytes 772
  1.8 0.7 %copy-start.4 = (s32[8]{0:T(128)S(1)}, s32[8]{0:T(128)}, u32[]{:S(2)}) copy-start(s32[8]{0:T(128)} %lengths.1) | copy-start | bytes 100
  1.9 0.7 %copy-start.5 = (f32[64]{0:T(128)S(1)}, f32[64]{0:T(128)}, u32[]{:S(2)}) copy-start(f32[64]{0:T(128)} %param.21) | copy-start | bytes 772
  1.9 0.7 %copy-start.6 = (f32[64]{0:T(128)S(1)}, f32[64]{0:T(128)}, u32[]{:S(2)}) copy-start(f32[64]{0:T(128)} %param.22) | copy-start | bytes 772

commit v4 on v3

--- a/solution.py
+++ b/solution.py
@@ -224,7 +224,7 @@
     def bc_params(tile):
         cols = slice((tile % groups) * TILE, (tile % groups + 1) * TILE)
         which = tile // groups
-        return wbc[:, tile * TILE : (tile + 1) * TILE].astype(F32), bbc[which : which + 1, cols]
+        return wbc[...].astype(F32)[:, which, cols], bbc[which : which + 1, cols]
 
     bc_tiles = 2 * bcols // TILE
     for tile in range(bc_tiles):
@@ -522,7 +522,7 @@
         bc_in.reshape(rows, bcw),
         wx,
         bx.reshape(1, chan),
-        wbc.reshape(width, bcw),
+        wbc,
         bbc,
         dt_raw,
         dt_bias.reshape(1, heads),

time: 36.8 us -> 36.8 us (level)
    unnamed x22 -> x21, local copies, waits for them, and re-layouts: 3.4 us -> 3.39 us
where the time goes in v4:
time: 36.8 us; the launch traced here: 36.6 us
  Pallas kernels  33 us (90%)
  local copies, waits for them, and re-layouts  3.39 us (9%)
    pallas_call x1, Pallas kernels, shards(): pl.pallas_call(functools.partial(kernel, peers), out_shape=jax.ShapeDtype...  33 us
    unnamed x21, local copies, waits for them, and re-layouts  3.39 us

profile of v4, /device:TPU:30, one launch (start us, length us, event | category | flops | bytes accessed | tf_op | source)
XLA Modules:
  0.0 36.6 jit_solution(18379471600325703755)
XLA Ops:
  0.0 0.8 %copy.14.dt = bf16[128,64]{1,0:T(8,128)(2,1)S(1)} copy(bf16[128,64]{0,1:T(8,128)(2,1)} %param.20) | data formatting | bytes 32768 | tf_op args[7]
  0.8 0.0 copy-start
  0.8 0.0 copy-start.1
  0.8 0.0 copy-start.2
  0.9 0.0 copy-start.3
  0.9 0.0 copy-start.4
  0.9 0.0 copy-start.8
  0.9 1.0 %copy.15 = bf16[16,8,2,256]{3,1,2,0:T(8,128)(2,1)S(1)} copy(bf16[16,8,2,256]{3,2,1,0:T(2,128)(2,1)} %bitcast.13) | data formatting | bytes 262144
  1.9 0.0 copy-start.5
  1.9 0.0 copy-start.6
  1.9 0.0 copy-start.7
  1.9 0.0 copy-done
  1.9 0.0 copy-done.1
  1.9 0.0 copy-done.2
  1.9 0.0 copy-done.3
  1.9 0.0 copy-done.4
  1.9 0.0 copy-done.8
  1.9 0.6 %copy-done.5 = s32[8]{0:T(128)S(1)} copy-done((s32[8]{0:T(128)S(1)}, s32[8]{0:T(128)}, u32[]{:S(2)}) %copy-start.5) | copy-done | bytes 56
  2.5 0.0 copy-done.6
  2.5 0.0 copy-done.7
  2.5 33.0 %mixer.1 = bf16[128,4096]{1,0:T(8,128)(2,1)S(1)} custom-call(s32[8]{0:T(128)S(1)} %copy-done.5, bf16[128,4096]{1,0:T(8,128)(2,1)} %x_hbm.1, bf16[128,4096]{1,0:T(8,128)(2,1)} %z_hbm.1, bf16[128,512]{1,0:T(8,128)(2,1)S(1)} %bitcast.7, bf16[4,4096]{1,0:T(4,128)(2,1)S(1)} %copy-done, f32[1,4096]{1,0:T(1,128)S(1)} %bitcast.8, bf16[4,2,256]{2,1,0:T(2,128)(2,1)S(1)} %copy-done.3, ...), custom_call_target="tpu_custom_call" | custom-call | tf_op jit(solution)/shard_map/mixer/pallas_call | solution.py:469
  35.6 1.0 %copy.17 = bf16[128,4096]{1,0:T(8,128)(2,1)} copy(bf16[128,4096]{1,0:T(8,128)(2,1)S(1)} %mixer.1) | data formatting | bytes 2097152
Async XLA Ops:
  0.8 1.1 %copy-start = (bf16[4,4096]{1,0:T(4,128)(2,1)S(1)}, bf16[4,4096]{1,0:T(4,128)(2,1)}, u32[]{:S(2)}) copy-start(bf16[4,4096]{1,0:T(4,128)(2,1)} %wx.1) | copy-start | bytes 98308
  0.8 1.1 %copy-start.1 = (f32[4096]{0:T(1024)S(1)}, f32[4096]{0:T(1024)}, u32[]{:S(2)}) copy-start(f32[4096]{0:T(1024)} %param.17) | copy-start | bytes 49156
  0.8 1.1 %copy-start.2 = (f32[4096]{0:T(1024)S(1)}, f32[4096]{0:T(1024)}, u32[]{:S(2)}) copy-start(f32[4096]{0:T(1024)} %param.24) | copy-start | bytes 49156
  0.9 1.1 %copy-start.3 = (bf16[4,2,256]{2,1,0:T(2,128)(2,1)S(1)}, bf16[4,2,256]{2,1,0:T(2,128)(2,1)}, u32[]{:S(2)}) copy-start(bf16[4,2,256]{2,1,0:T(2,128)(2,1)} %wbc.1) | copy-start | bytes 12292
  0.9 1.1 %copy-start.4 = (f32[2,256]{1,0:T(2,128)S(1)}, f32[2,256]{1,0:T(2,128)}, u32[]{:S(2)}) copy-start(f32[2,256]{1,0:T(2,128)} %bbc.1) | copy-start | bytes 6148
  0.9 1.1 %copy-start.8 = (f32[64]{0:T(128)S(1)}, f32[64]{0:T(128)}, u32[]{:S(2)}) copy-start(f32[64]{0:T(128)} %param.23) | copy-start | bytes 772
  1.9 0.7 %copy-start.5 = (s32[8]{0:T(128)S(1)}, s32[8]{0:T(128)}, u32[]{:S(2)}) copy-start(s32[8]{0:T(128)} %lengths.1) | copy-start | bytes 100
  1.9 0.7 %copy-start.6 = (f32[64]{0:T(128)S(1)}, f32[64]{0:T(128)}, u32[]{:S(2)}) copy-start(f32[64]{0:T(128)} %param.21) | copy-start | bytes 772
  1.9 0.7 %copy-start.7 = (f32[64]{0:T(128)S(1)}, f32[64]{0:T(128)}, u32[]{:S(2)}) copy-start(f32[64]{0:T(128)} %param.22) | copy-start | bytes 772
